TPU v7x, 32 devices: a whole 2x2x4 slice. The times are simulated.
32 devices in a mesh: ctx: 8 (over z, y), help: 4 (over x, core).
Axes of the slice: x: 2, y: 2, z: 4, core: 2. Of those that a mesh axis runs over, the one named last changes fastest.
Arguments:
- query_rows: bfloat16 [1, 8192, 2048], P(None, ('ctx', 'help')), may hold values from -126 to 126
- key_rows: bfloat16 [1, 8192, 2048], P(None, 'ctx'), may hold values from -6.5 to 6.5
- value_rows: bfloat16 [1, 8192, 2048], P(None, 'ctx'), may hold values from -6 to 6
- output_grad: bfloat16 [1, 8192, 2048], P(None, ('ctx', 'help')), may hold values from -96 to 96
- block_choice: int32 [1, 8192, 2], P(None, ('ctx', 'help')), may hold values from 0 to 7, as said below
Outputs:
- query_grad: bfloat16 [1, 8192, 2048], P(None, ('ctx', 'help'))
- key_grad: bfloat16 [1, 8192, 2048], P(None, ('ctx', 'help'))
- value_grad: bfloat16 [1, 8192, 2048], P(None, ('ctx', 'help'))
Inputs may be any that keep to these rules, and one draw needn't show every extreme that they name: `block_choice`: an entry names a block only where it is below the token's own block index; the entries of a token that name blocks name different blocks. In each aligned run of 256 rows of one sequence (the rows of one device) no block is named more than 64 times, and the devices of a sequence's third block name each of its first two blocks exactly 64 times. Blocks early in a sequence are named by the tokens of more blocks than late ones.
All inputs are finite; a program needn't handle non-finite values.
Results may differ from a plain program's by a relative error of at most 0.01.
Values may be sent and summed in bfloat16 or wider, within the bound.
A program may use at most 192 MiB of HBM per device.

v0:
```python
import math

import jax
import jax.numpy as jnp
from jax import lax
from jax.sharding import PartitionSpec as P

HEAD_DIM = 128


NEGATIVE = -1e30


def head_part(matrix, start_col, group_heads):
    sliced = matrix[:, :, start_col : start_col + group_heads * HEAD_DIM]
    return sliced.reshape(matrix.shape[0], matrix.shape[1], group_heads, HEAD_DIM)


def mask_of(limits, key_count):
    return jnp.arange(key_count, dtype=jnp.int32)[None, :] <= limits[:, None]


def block_statistics(queries, grads_out, key_block, value_block, limits, group_heads):
    features = queries.shape[2]
    allowed = mask_of(limits, key_block.shape[1])
    scaling = HEAD_DIM ** (-0.5)
    maxima_list = []
    norm_list = []
    intersection_list = []
    for counter in range(features // (group_heads * HEAD_DIM)):
        start_col = counter * group_heads * HEAD_DIM
        scores = (
            jnp.einsum(
                "srhd,skhd->shrk",
                head_part(queries, start_col, group_heads),
                head_part(key_block, start_col, group_heads),
                preferred_element_type=jnp.float32,
            )
            * scaling
        )
        scores = jnp.where(allowed, scores, NEGATIVE)
        highest = jnp.max(scores, axis=3)
        weights = jnp.where(allowed, jnp.exp(scores - highest[..., None]), 0.0)
        products = jnp.einsum(
            "srhd,skhd->shrk",
            head_part(grads_out, start_col, group_heads),
            head_part(value_block, start_col, group_heads),
            preferred_element_type=jnp.float32,
        )
        maxima_list.append(highest)
        norm_list.append(jnp.sum(weights, axis=3))
        intersection_list.append(jnp.sum(weights * products, axis=3))
    return (
        jnp.concatenate(maxima_list, axis=1),
        jnp.concatenate(norm_list, axis=1),
        jnp.concatenate(intersection_list, axis=1),
    )


def block_gradients(
    queries, grads_out, key_block, value_block, limits, log_rows, shift_rows, group_heads
):
    seq_count, row_total, features = queries.shape
    key_count = key_block.shape[1]
    allowed = mask_of(limits, key_count)
    scaling = HEAD_DIM ** (-0.5)
    width_part = group_heads * HEAD_DIM
    query_list = []
    key_list = []
    value_list = []
    for counter in range(features // width_part):
        start_col = counter * width_part
        head_start = counter * group_heads
        query_part = head_part(queries, start_col, group_heads)
        key_part = head_part(key_block, start_col, group_heads)
        grad_part = head_part(grads_out, start_col, group_heads)
        value_part = head_part(value_block, start_col, group_heads)
        log_part = log_rows[:, head_start : head_start + group_heads, :]
        shift_part = shift_rows[:, head_start : head_start + group_heads, :]
        scores = (
            jnp.einsum("srhd,skhd->shrk", query_part, key_part, preferred_element_type=jnp.float32)
            * scaling
        )
        probabilities = jnp.where(allowed, jnp.exp(scores - log_part[..., None]), 0.0)
        products = jnp.einsum(
            "srhd,skhd->shrk", grad_part, value_part, preferred_element_type=jnp.float32
        )
        prob_low = probabilities.astype(jnp.bfloat16)
        mixed_low = (probabilities * (products - shift_part[..., None])).astype(jnp.bfloat16)
        value_new = jnp.einsum(
            "shrk,srhd->skhd", prob_low, grad_part, preferred_element_type=jnp.float32
        )
        key_new = (
            jnp.einsum("shrk,srhd->skhd", mixed_low, query_part, preferred_element_type=jnp.float32)
            * scaling
        )
        query_new = (
            jnp.einsum("shrk,skhd->srhd", mixed_low, key_part, preferred_element_type=jnp.float32)
            * scaling
        )
        query_list.append(query_new.reshape(seq_count, row_total, width_part))
        key_list.append(key_new.reshape(seq_count, key_count, width_part))
        value_list.append(value_new.reshape(seq_count, key_count, width_part))
    return (
        jnp.concatenate(query_list, axis=2),
        jnp.concatenate(key_list, axis=2),
        jnp.concatenate(value_list, axis=2),
    )


def slot_layout(block_choice, center, blocks, capacity):
    present = block_choice < center
    targets = jnp.where(present, center - 1 - block_choice, -1)
    matches = (targets[..., None] == jnp.arange(blocks, dtype=jnp.int32)).astype(jnp.int32)
    counts = jnp.sum(matches, axis=2)
    earlier = jnp.cumsum(counts, axis=1) - counts
    places = jnp.sum(matches * earlier[:, :, None, :], axis=3)
    slot_ids = jnp.where(present, targets * capacity + places, 0)
    selector = (
        (slot_ids[..., None] == jnp.arange(blocks * capacity, dtype=jnp.int32)) & present[..., None]
    ).astype(jnp.float32)
    picker = jnp.sum(selector, axis=2)
    return (selector, picker, present)


def per_device(query_rows, key_rows, value_rows, output_grad, block_choice):
    blocks = lax.axis_size("ctx")
    center = lax.axis_index("ctx")
    helper = lax.axis_index("help")
    seq_count, rows_dev, features = query_rows.shape
    routed = block_choice.shape[2]
    block_len = key_rows.shape[1]
    head_count = features // HEAD_DIM
    capacity = 2 * max(1, rows_dev // blocks)
    slot_total = blocks * capacity
    group_heads = math.gcd(head_count, 4)
    selector, picker, present = slot_layout(block_choice, center, blocks, capacity)
    picker_low = picker.astype(jnp.bfloat16)
    own_limits = helper * rows_dev + jnp.arange(rows_dev, dtype=jnp.int32)
    limits = jnp.concatenate([own_limits, jnp.full((slot_total,), block_len - 1, jnp.int32)])

    def pack_rows(source):
        packed = jnp.einsum(
            "stu,stw->suw", picker_low, source, preferred_element_type=jnp.float32
        ).astype(jnp.bfloat16)
        return packed.reshape(seq_count, blocks, capacity, features)

    def join_rows(own, received):
        return jnp.concatenate([own, received.reshape(seq_count, slot_total, features)], axis=1)

    got_queries, got_grads = (
        lax.all_to_all(pack_rows(query_rows), "ctx", split_axis=1, concat_axis=1, tiled=True),
        lax.all_to_all(pack_rows(output_grad), "ctx", split_axis=1, concat_axis=1, tiled=True),
    )
    all_queries = join_rows(query_rows, got_queries)
    all_grads = join_rows(output_grad, got_grads)
    maxima, normalizers, intersections = block_statistics(
        all_queries, all_grads, key_rows, value_rows, limits, group_heads
    )

    def routed_part(statistic):
        routed_tail = statistic[:, :, rows_dev:].reshape(seq_count, head_count, blocks, capacity)
        return jnp.transpose(routed_tail, (0, 2, 1, 3))

    back_max, back_norm, back_dot = (
        lax.all_to_all(routed_part(maxima), "ctx", split_axis=1, concat_axis=1, tiled=True),
        lax.all_to_all(routed_part(normalizers), "ctx", split_axis=1, concat_axis=1, tiled=True),
        lax.all_to_all(routed_part(intersections), "ctx", split_axis=1, concat_axis=1, tiled=True),
    )

    def unpack_stat(stat_back, route_index, filler):
        flattened = jnp.transpose(stat_back, (0, 2, 1, 3)).reshape(
            seq_count, head_count, slot_total
        )
        picked = jnp.einsum(
            "stu,shu->sht",
            selector[:, :, route_index, :],
            flattened,
            precision=lax.Precision.HIGHEST,
        )
        return jnp.where(present[:, None, :, route_index], picked, filler)

    portions = [
        (maxima[:, :, :rows_dev], normalizers[:, :, :rows_dev], intersections[:, :, :rows_dev])
    ]
    for route_index in range(routed):
        portions.append(
            (
                unpack_stat(back_max, route_index, NEGATIVE),
                unpack_stat(back_norm, route_index, 0.0),
                unpack_stat(back_dot, route_index, 0.0),
            )
        )
    top_value = portions[0][0]
    for portion in portions[1:]:
        top_value = jnp.maximum(top_value, portion[0])
    norm_total = jnp.zeros_like(top_value)
    dot_total = jnp.zeros_like(top_value)
    for portion in portions:
        factor = jnp.exp(portion[0] - top_value)
        norm_total = norm_total + portion[1] * factor
        dot_total = dot_total + portion[2] * factor
    log_total = top_value + jnp.log(norm_total)
    centering = dot_total / norm_total

    def pack_stat(statistic):
        spread = jnp.einsum("stu,sht->shu", picker, statistic, precision=lax.Precision.HIGHEST)
        return jnp.transpose(spread.reshape(seq_count, head_count, blocks, capacity), (0, 2, 1, 3))

    def join_stat(own, received):
        moved_stat = jnp.transpose(received, (0, 2, 1, 3)).reshape(
            seq_count, head_count, slot_total
        )
        return jnp.concatenate([own, moved_stat], axis=2)

    got_logs, got_shifts = (
        lax.all_to_all(pack_stat(log_total), "ctx", split_axis=1, concat_axis=1, tiled=True),
        lax.all_to_all(pack_stat(centering), "ctx", split_axis=1, concat_axis=1, tiled=True),
    )
    log_all = join_stat(log_total, got_logs)
    shift_all = join_stat(centering, got_shifts)
    query_terms, key_terms, value_terms = block_gradients(
        all_queries, all_grads, key_rows, value_rows, limits, log_all, shift_all, group_heads
    )
    key_sum, value_sum = (
        lax.psum_scatter(
            key_terms.astype(jnp.bfloat16), "help", scatter_dimension=1, tiled=True
        ).astype(jnp.float32),
        lax.psum_scatter(
            value_terms.astype(jnp.bfloat16), "help", scatter_dimension=1, tiled=True
        ).astype(jnp.float32),
    )
    key_out = key_sum.astype(jnp.bfloat16)
    value_out = value_sum.astype(jnp.bfloat16)
    returned = lax.all_to_all(
        query_terms[:, rows_dev:, :]
        .reshape(seq_count, blocks, capacity, features)
        .astype(jnp.bfloat16),
        "ctx",
        split_axis=1,
        concat_axis=1,
        tiled=True,
    ).astype(jnp.float32)
    flattened = returned.reshape(seq_count, slot_total, features)
    gathered_terms = jnp.einsum("stu,suw->stw", picker, flattened, precision=lax.Precision.HIGHEST)
    summed = query_terms[:, :rows_dev, :] + gathered_terms
    return (summed.astype(jnp.bfloat16), key_out, value_out)


def solution(mesh):
    placed = (
        P(None, ("ctx", "help"), None),
        P(None, "ctx", None),
        P(None, "ctx", None),
        P(None, ("ctx", "help"), None),
        P(None, ("ctx", "help"), None),
    )
    return jax.shard_map(
        per_device,
        mesh=mesh,
        in_specs=placed,
        out_specs=(
            P(None, ("ctx", "help"), None),
            P(None, ("ctx", "help"), None),
            P(None, ("ctx", "help"), None),
        ),
        check_vma=False,
    )
```

profile of v0, /device:TPU:0, one launch (start us, length us, event | category | flops | bytes accessed | tf_op | source)
XLA Modules:
  0.0 506.0 jit_solution(13670169112367688720)
XLA Ops:
  9.8 3.5 convolution_convert_fusion.1
  13.3 7.3 %all-to-all-start = ((bf16[1,8,64,2048]{3,2,0,1:T(8,128)(2,1)}), bf16[1,8,64,2048]{3,2,0,1:T(8,128)(2,1)S(1)}, u32[]{:S(2)}, u32[]{:S(2)}) async-start(bf16[1,8,64,2048]{3,2,0,1:T(8,128)(2,1)} %bitcast.353), calls=%async_computation | async-start | bytes 4194304 | tf_op jit(solution)/shard_map/all_to_all | solution.py:152
  20.5 3.3 convolution_convert_fusion
  23.8 45.0 %all-to-all-done = bf16[1,8,64,2048]{3,2,0,1:T(8,128)(2,1)S(1)} async-done(((bf16[1,8,64,2048]{3,2,0,1:T(8,128)(2,1)}), bf16[1,8,64,2048]{3,2,0,1:T(8,128)(2,1)S(1)}, u32[]{:S(2)}, u32[]{:S(2)}) %all-to-all-start) | async-done | bytes 2097184 | tf_op jit(solution)/shard_map/all_to_all | solution.py:152
  68.8 4.3 all-to-all-start.4
  73.1 4.3 fusion.89
  86.5 4.3 fusion.88
  97.6 2.5 copy.324
  103.0 3.0 fusion.55
  113.1 7.8 %all-to-all-done.4 = bf16[1,8,64,2048]{3,2,0,1:T(8,128)(2,1)} async-done(((bf16[1,8,64,2048]{3,2,0,1:T(8,128)(2,1)}), bf16[1,8,64,2048]{3,2,0,1:T(8,128)(2,1)}, u32[]{:S(2)}, u32[]{:S(2)}) %all-to-all-start.4) | async-done | bytes 2097184 | tf_op jit(solution)/shard_map/all_to_all | solution.py:153
  121.0 3.6 fusion.52
  133.7 7.6 %fusion.100 = f32[4,768,1024]{2,1,0:T(8,128)} fusion(bf16[768,4,128]{0,2,1:T(8,128)(2,1)S(1)} %bitcast.347, bf16[1024,4,128]{0,2,1:T(8,128)(2,1)} %bitcast.360), kind=kOutput, calls=%fused_computation.198 | convolution fusion | flops 805306368 | bytes 14417920 | tf_op jit(solution)/shard_map/srhd,skhd->shrk/dot_general | solution.py:33
  141.4 6.4 %fusion.101 = f32[4,768,1024]{2,1,0:T(8,128)} fusion(bf16[768,4,128]{0,2,1:T(8,128)(2,1)S(1)} %bitcast.345, bf16[1024,4,128]{0,2,1:T(8,128)(2,1)S(1)} %bitcast.358), kind=kOutput, calls=%fused_computation.199 | convolution fusion | flops 805306368 | bytes 14417920 | tf_op jit(solution)/shard_map/srhd,skhd->shrk/dot_general | solution.py:33
  147.8 6.4 %fusion.99 = f32[4,768,1024]{2,1,0:T(8,128)} fusion(bf16[768,4,128]{0,2,1:T(8,128)(2,1)S(1)} %bitcast.349, bf16[1024,4,128]{0,2,1:T(8,128)(2,1)S(1)} %bitcast.362), kind=kOutput, calls=%fused_computation.197 | convolution fusion | flops 805306368 | bytes 14417920 | tf_op jit(solution)/shard_map/srhd,skhd->shrk/dot_general | solution.py:33
  154.2 6.3 %fusion.102 = f32[4,768,1024]{2,1,0:T(8,128)} fusion(bf16[768,4,128]{0,2,1:T(8,128)(2,1)S(1)} %bitcast.369, bf16[1024,4,128]{0,2,1:T(8,128)(2,1)S(1)} %bitcast.364), kind=kOutput, calls=%fused_computation.200 | convolution fusion | flops 805306368 | bytes 14417920 | tf_op jit(solution)/shard_map/srhd,skhd->shrk/dot_general | solution.py:44
  160.5 6.3 %fusion.103 = f32[4,768,1024]{2,1,0:T(8,128)} fusion(bf16[768,4,128]{0,2,1:T(8,128)(2,1)S(1)} %bitcast.366, bf16[1024,4,128]{0,2,1:T(8,128)(2,1)S(1)} %bitcast.365), kind=kOutput, calls=%fused_computation.201 | convolution fusion | flops 805306368 | bytes 14417920 | tf_op jit(solution)/shard_map/srhd,skhd->shrk/dot_general | solution.py:44
  166.8 7.6 %select_reduce_fusion.3 = (f32[4,768]{1,0:T(4,128)S(1)}, f32[4,768,1024]{2,1,0:T(8,128)}) fusion(pred[768,1024]{1,0:T(8,128)(4,1)S(1)} %iota_compare_fusion, bf16[768,4,128]{0,2,1:T(8,128)(2,1)S(1)} %bitcast.356, bf16[1024,4,128]{0,2,1:T(8,128)(2,1)S(1)} %bitcast.377), kind=kOutput, calls=%fused_computation.19 | convolution fusion | flops 814740480 | bytes 15216640 | tf_op jit(solution)/shard_map/srhd,skhd->shrk/dot_general | solution.py:81
  174.4 24.9 %multiply_reduce_fusion.3 = (f32[4,768]{1,0:T(4,128)}, f32[4,768]{1,0:T(4,128)S(1)}, f32[4,768]{1,0:T(4,128)S(1)}, f32[4,768]{1,0:T(4,128)S(1)}, f32[4,768]{1,0:T(4,128)S(1)}, /*index=5*/f32[4,768,1024]{2,1,0:T(8,128)}) fusion(f32[4,768,1024]{2,1,0:T(8,128)} %get-tuple-element.51, f32[4,768]{1,0:T(4,128)S(1)} %get-tuple-element.50, ...), kind=kOutput, calls=%fused_computation.10 | convolution fusion | flops 855622656 | bytes 65609728 | tf_op jit(solution)/shard_map/srhd,skhd->shrk/dot_general | solution.py:85
  199.4 30.2 %multiply_reduce_fusion.2 = (f32[4,768]{1,0:T(4,128)}, f32[4,768]{1,0:T(4,128)S(1)}, f32[4,768]{1,0:T(4,128)S(1)}, f32[4,768]{1,0:T(4,128)}, f32[4,768]{1,0:T(4,...) fusion(f32[4,768,1024]{2,1,0:T(8,128)} %fusion.99, f32[4,768]{1,0:T(4,128)S(1)} %get-tuple-element.11, ...), kind=kOutput, calls=%fused_computation.9 | convolution fusion | flops 871348224 | bytes 78229504 | tf_op jit(solution)/shard_map/srhd,skhd->shrk/dot_general | solution.py:44
  231.0 4.0 all-to-all-start.2
  241.7 3.8 all-to-all-start.1
  248.3 3.9 all-to-all-done.1
  252.8 3.3 all-to-all-start.5
  263.8 5.9 %all-to-all-start.3 = ((f32[8,1,1024]{2,1,0:T(1,128)}), f32[8,1,1024]{2,1,0:T(1,128)S(1)}, u32[]{:S(2)}, u32[]{:S(2)}) async-start(f32[8,1,1024]{2,1,0:T(1,128)} %reshape.757), calls=%async_computation.3 | async-start | bytes 65536 | tf_op jit(solution)/shard_map/all_to_all | solution.py:217
  276.5 5.0 all-to-all-start.6
  282.4 5.7 %all-to-all-done.6 = f32[8,1,1024]{2,1,0:T(1,128)S(1)} async-done(((f32[8,1,1024]{2,1,0:T(1,128)}), f32[8,1,1024]{2,1,0:T(1,128)S(1)}, u32[]{:S(2)}, u32[]{:S(2)}) %all-to-all-start.6) | async-done | bytes 32800 | tf_op jit(solution)/shard_map/all_to_all | solution.py:218
  289.1 8.8 %fusion.22 = bf16[4,128,1024]{2,1,0:T(8,128)(2,1)} fusion(bf16[768,4,128]{0,2,1:T(8,128)(2,1)} %bitcast.388, f32[4,768,1024]{2,1,0:T(8,128)} %get-tuple-element.51, f32[4,768]{1,0:T(4,128)S(1)} %get-tuple-element.59, pred[768,1024]{1,0:T(8,128)(4,1)S(1)} %iota_compare_fusion), kind=kOutput, calls=%fused_computation.62 | convolution fusion | flops 818413568 | bytes 15216640 | tf_op jit(solution)/shard_map/shrk,srhd->skhd/dot_general | solution.py:90
  300.1 8.8 %fusion.25 = bf16[4,128,1024]{2,1,0:T(8,128)(2,1)} fusion(bf16[768,4,128]{0,2,1:T(8,128)(2,1)} %bitcast.391, f32[4,768,1024]{2,1,0:T(8,128)} %fusion.99, f32[4,768]{1,0:T(4,128)S(1)} %get-tuple-element.58, pred[768,1024]{1,0:T(8,128)(4,1)S(1)} %iota_compare_fusion), kind=kOutput, calls=%fused_computation.63 | convolution fusion | flops 818413568 | bytes 15216640 | tf_op jit(solution)/shard_map/shrk,srhd->skhd/dot_general | solution.py:90
  311.2 8.8 %fusion.28 = bf16[4,128,1024]{2,1,0:T(8,128)(2,1)} fusion(bf16[768,4,128]{0,2,1:T(8,128)(2,1)} %bitcast.368, f32[4,768,1024]{2,1,0:T(8,128)} %fusion.100, f32[4,768]{1,0:T(4,128)S(1)} %get-tuple-element.56, pred[768,1024]{1,0:T(8,128)(4,1)S(1)} %iota_compare_fusion), kind=kOutput, calls=%fused_computation.64 | convolution fusion | flops 818413568 | bytes 15216640 | tf_op jit(solution)/shard_map/shrk,srhd->skhd/dot_general | solution.py:90
  322.3 7.4 %fusion.31 = bf16[4,128,1024]{2,1,0:T(8,128)(2,1)} fusion(bf16[768,4,128]{0,2,1:T(8,128)(2,1)S(1)} %bitcast.367, f32[4,768,1024]{2,1,0:T(8,128)} %fusion.101, f32[4,768]{1,0:T(4,128)S(1)} %get-tuple-element.57, pred[768,1024]{1,0:T(8,128)(4,1)S(1)} %iota_compare_fusion), kind=kOutput, calls=%fused_computation.65 | convolution fusion | flops 818413568 | bytes 15216640 | tf_op jit(solution)/shard_map/shrk,srhd->skhd/dot_general | solution.py:90
  332.0 3.7 pad_maximum_fusion.2
  336.0 42.9 %multiply_convert_fusion.3 = (bf16[4,768,1024]{2,1,0:T(8,128)(2,1)S(1)}, bf16[4,768,1024]{2,1,0:T(8,128)(2,1)}, bf16[4,768,1024]{2,1,0:T(8,128)(2,1)}, bf16[4,768,1024]{2,1,0:T(8,128)(2,1)}) fusion(f32[4,768,1024]{2,1,0:T(8,128)} %get-tuple-element.52, f32[4,768,1024]{2,1,0:T(8,128)} %get-tuple-element.51, f32[4,768]{1,0:T(4,128)S(1)} %get-tuple-element.46, ...), kind=kLoop, calls=%fused_computation.6 | loop fusion | flops 75497472 | bytes 126713856 | tf_op jit(solution)/shard_map/convert_element_type | solution.py:89
  378.9 2.7 copy-done
  385.2 4.8 multiply_convert_fusion.6
  392.4 4.8 multiply_convert_fusion.5
  397.1 2.4 copy.297
  399.5 4.8 multiply_convert_fusion.4
  406.6 4.4 pad_maximum_fusion.1
  411.0 5.6 %convolution_multiply_fusion.3 = f32[4,768,128]{1,2,0:T(8,128)S(1)} fusion(bf16[4,768,1024]{2,1,0:T(8,128)(2,1)} %copy-done, bf16[1024,4,128]{0,2,1:T(8,128)(2,1)} %bitcast.376), kind=kOutput, calls=%fused_computation.69 | convolution fusion | flops 805699584 | bytes 8912896 | tf_op jit(solution)/shard_map/shrk,skhd->srhd/dot_general | solution.py:98
  418.3 6.4 %convolution_multiply_fusion.2 = f32[4,768,128]{1,2,0:T(8,128)} fusion(bf16[4,768,1024]{2,1,0:T(8,128)(2,1)} %get-tuple-element.41, bf16[1024,4,128]{0,2,1:T(8,128)(2,1)S(1)} %bitcast.363), kind=kOutput, calls=%fused_computation.68 | convolution fusion | flops 805699584 | bytes 8912896 | tf_op jit(solution)/shard_map/shrk,skhd->srhd/dot_general | solution.py:98
  424.7 3.0 copy.291
  427.8 6.3 %convolution_multiply_fusion.1 = f32[4,768,128]{1,2,0:T(8,128)} fusion(bf16[4,768,1024]{2,1,0:T(8,128)(2,1)} %get-tuple-element.39, bf16[1024,4,128]{0,2,1:T(8,128)(2,1)S(1)} %bitcast.361), kind=kOutput, calls=%fused_computation.67 | convolution fusion | flops 805699584 | bytes 8912896 | tf_op jit(solution)/shard_map/shrk,skhd->srhd/dot_general | solution.py:98
  434.0 3.0 copy.292
  437.0 6.2 %convolution_multiply_fusion = f32[4,768,128]{1,2,0:T(8,128)} fusion(bf16[4,768,1024]{2,1,0:T(8,128)(2,1)} %get-tuple-element.40, bf16[1024,4,128]{0,2,1:T(8,128)(2,1)S(1)} %bitcast.359), kind=kOutput, calls=%fused_computation.66 | convolution fusion | flops 805699584 | bytes 8912896 | tf_op jit(solution)/shard_map/shrk,skhd->srhd/dot_general | solution.py:98
  443.3 3.1 copy.293
  446.4 2.7 pad_maximum_fusion
  449.4 46.4 %all_to_all.40 = bf16[1,8,64,2048]{3,2,0,1:T(8,128)(2,1)S(1)} all-to-all(bf16[1,8,64,2048]{3,2,0,1:T(8,128)(2,1)S(1)} %bitcast.354), channel_id=1, replica_groups=mesh['ctx'=8,'help'=4] {'ctx'}, dimensions={1} | all-to-all | bytes 4194304 | tf_op jit(solution)/shard_map/all_to_all | solution.py:235
  495.8 2.9 fusion.21
  (161 shorter events, 85.0 us)
Async XLA Ops:
  9.7 90.3 %copy-start.1 = (f32[256,512]{1,0:T(8,128)}, f32[256,512]{1,0:T(8,128)S(1)}, u32[]{:S(2)}) copy-start(f32[256,512]{1,0:T(8,128)S(1)} %convert_reduce_fusion) | copy-start | bytes 1572868
  13.3 55.5 %all-to-all-start = ((bf16[1,8,64,2048]{3,2,0,1:T(8,128)(2,1)}), bf16[1,8,64,2048]{3,2,0,1:T(8,128)(2,1)S(1)}, u32[]{:S(2)}, u32[]{:S(2)}) async-start(bf16[1,8,64,2048]{3,2,0,1:T(8,128)(2,1)} %bitcast.353), calls=%async_computation | async-start | bytes 4194304 | tf_op jit(solution)/shard_map/all_to_all | solution.py:152
  68.8 52.2 %all-to-all-start.4 = ((bf16[1,8,64,2048]{3,2,0,1:T(8,128)(2,1)}), bf16[1,8,64,2048]{3,2,0,1:T(8,128)(2,1)}, u32[]{:S(2)}, u32[]{:S(2)}) async-start(bf16[1,8,64,2048]{3,2,0,1:T(8,128)(2,1)} %bitcast.352), calls=%async_computation.4 | async-start | bytes 4194304 | tf_op jit(solution)/shard_map/all_to_all | solution.py:153
  109.7 24.0 %copy-start.5 = (bf16[1,768,512]{1,2,0:T(8,128)(2,1)}, bf16[1,768,512]{1,2,0:T(8,128)(2,1)S(1)}, u32[]{:S(2)}) copy-start(bf16[1,768,512]{1,2,0:T(8,128)(2,1)S(1)} %copy.254) | copy-start | bytes 2359300
  111.4 29.9 %copy-start.3 = (bf16[1,768,512]{1,2,0:T(8,128)(2,1)}, bf16[1,768,512]{1,2,0:T(8,128)(2,1)S(1)}, u32[]{:S(2)}) copy-start(bf16[1,768,512]{1,2,0:T(8,128)(2,1)S(1)} %copy.258) | copy-start | bytes 2359300
  133.7 7.6 %copy-start.8 = (bf16[1,1024,512]{1,2,0:T(8,128)(2,1)S(1)}, bf16[1,1024,512]{1,2,0:T(8,128)(2,1)}, u32[]{:S(2)}) copy-start(bf16[1,1024,512]{1,2,0:T(8,128)(2,1)} %copy.322) | copy-start | bytes 3145732
  141.4 6.4 %copy-start.11 = (bf16[1,1024,512]{1,2,0:T(8,128)(2,1)S(1)}, bf16[1,1024,512]{1,2,0:T(8,128)(2,1)}, u32[]{:S(2)}) copy-start(bf16[1,1024,512]{1,2,0:T(8,128)(2,1)} %copy.320) | copy-start | bytes 3145732
  147.8 6.4 %copy-start.13 = (bf16[1,1024,512]{1,2,0:T(8,128)(2,1)S(1)}, bf16[1,1024,512]{1,2,0:T(8,128)(2,1)}, u32[]{:S(2)}) copy-start(bf16[1,1024,512]{1,2,0:T(8,128)(2,1)} %copy.325) | copy-start | bytes 3145732
  147.8 6.4 %copy-start.17 = (bf16[1,768,512]{1,2,0:T(8,128)(2,1)S(1)}, bf16[1,768,512]{1,2,0:T(8,128)(2,1)}, u32[]{:S(2)}) copy-start(bf16[1,768,512]{1,2,0:T(8,128)(2,1)} %copy.278) | copy-start | bytes 2359300
  154.2 6.3 %copy-start.14 = (bf16[1,1024,512]{1,2,0:T(8,128)(2,1)S(1)}, bf16[1,1024,512]{1,2,0:T(8,128)(2,1)}, u32[]{:S(2)}) copy-start(bf16[1,1024,512]{1,2,0:T(8,128)(2,1)} %copy.326) | copy-start | bytes 3145732
  154.2 6.3 %copy-start.16 = (bf16[1,768,512]{1,2,0:T(8,128)(2,1)S(1)}, bf16[1,768,512]{1,2,0:T(8,128)(2,1)}, u32[]{:S(2)}) copy-start(bf16[1,768,512]{1,2,0:T(8,128)(2,1)} %copy.282) | copy-start | bytes 2359300
  160.5 6.3 %copy-start.7 = (bf16[1,768,512]{1,2,0:T(8,128)(2,1)S(1)}, bf16[1,768,512]{1,2,0:T(8,128)(2,1)}, u32[]{:S(2)}) copy-start(bf16[1,768,512]{1,2,0:T(8,128)(2,1)} %copy.246) | copy-start | bytes 2359300
  160.5 6.3 %copy-start.19 = (bf16[1,1024,512]{1,2,0:T(8,128)(2,1)S(1)}, bf16[1,1024,512]{1,2,0:T(8,128)(2,1)}, u32[]{:S(2)}) copy-start(bf16[1,1024,512]{1,2,0:T(8,128)(2,1)} %copy.319) | copy-start | bytes 3145732
  166.8 7.6 %copy-start.20 = (bf16[1,1024,512]{1,2,0:T(8,128)(2,1)S(1)}, bf16[1,1024,512]{1,2,0:T(8,128)(2,1)}, u32[]{:S(2)}) copy-start(bf16[1,1024,512]{1,2,0:T(8,128)(2,1)} %copy.323) | copy-start | bytes 3145732
  166.8 7.6 %copy-start.21 = (bf16[1,768,512]{1,2,0:T(8,128)(2,1)S(1)}, bf16[1,768,512]{1,2,0:T(8,128)(2,1)}, u32[]{:S(2)}) copy-start(bf16[1,768,512]{1,2,0:T(8,128)(2,1)} %copy.270) | copy-start | bytes 2359300
  199.3 30.2 %copy-start.24 = (f32[4,768]{1,0:T(4,128)}, f32[4,768]{1,0:T(4,128)S(1)}, u32[]{:S(2)}) copy-start(f32[4,768]{1,0:T(4,128)S(1)} %get-tuple-element.11) | copy-start | bytes 36868
  199.3 30.2 %copy-start.25 = (f32[4,768]{1,0:T(4,128)}, f32[4,768]{1,0:T(4,128)S(1)}, u32[]{:S(2)}) copy-start(f32[4,768]{1,0:T(4,128)S(1)} %get-tuple-element.12) | copy-start | bytes 36868
  199.3 30.2 %copy-start.26 = (f32[4,768]{1,0:T(4,128)}, f32[4,768]{1,0:T(4,128)S(1)}, u32[]{:S(2)}) copy-start(f32[4,768]{1,0:T(4,128)S(1)} %get-tuple-element.13) | copy-start | bytes 36868
  199.4 30.3 %copy-start.27 = (f32[4,768]{1,0:T(4,128)}, f32[4,768]{1,0:T(4,128)S(1)}, u32[]{:S(2)}) copy-start(f32[4,768]{1,0:T(4,128)S(1)} %get-tuple-element.4) | copy-start | bytes 36868
  199.4 58.4 %copy-start.22 = (pred[1,256,2,512]{3,1,2,0:T(32,128)(4,1)S(1)}, pred[1,256,2,512]{3,1,2,0:T(32,128)(4,1)}, u32[]{:S(2)}) copy-start(pred[1,256,2,512]{3,1,2,0:T(32,128)(4,1)} %fusion.51) | copy-start | bytes 786436
  229.6 0.6 copy-start.28
  229.6 0.6 copy-start.29
  229.6 0.6 copy-start.30
  231.0 10.7 %all-to-all-start.2 = ((f32[8,1,1024]{2,1,0:T(1,128)}), f32[8,1,1024]{2,1,0:T(1,128)}, u32[]{:S(2)}, u32[]{:S(2)}) async-start(f32[8,1,1024]{2,1,0:T(1,128)} %reshape.749), calls=%async_computation.2 | async-start | bytes 65536 | tf_op jit(solution)/shard_map/all_to_all | solution.py:167
  241.7 10.5 %all-to-all-start.1 = ((f32[8,1,1024]{2,1,0:T(1,128)}), f32[8,1,1024]{2,1,0:T(1,128)S(1)}, u32[]{:S(2)}, u32[]{:S(2)}) async-start(f32[8,1,1024]{2,1,0:T(1,128)} %reshape.751), calls=%async_computation.1 | async-start | bytes 65536 | tf_op jit(solution)/shard_map/all_to_all | solution.py:166
  252.2 0.6 copy-start.23
  252.8 11.0 %all-to-all-start.5 = ((f32[8,1,1024]{2,1,0:T(1,128)}), f32[8,1,1024]{2,1,0:T(1,128)S(1)}, u32[]{:S(2)}, u32[]{:S(2)}) async-start(f32[8,1,1024]{2,1,0:T(1,128)} %reshape.753), calls=%async_computation.5 | async-start | bytes 65536 | tf_op jit(solution)/shard_map/all_to_all | solution.py:168
  263.8 12.6 %all-to-all-start.3 = ((f32[8,1,1024]{2,1,0:T(1,128)}), f32[8,1,1024]{2,1,0:T(1,128)S(1)}, u32[]{:S(2)}, u32[]{:S(2)}) async-start(f32[8,1,1024]{2,1,0:T(1,128)} %reshape.757), calls=%async_computation.3 | async-start | bytes 65536 | tf_op jit(solution)/shard_map/all_to_all | solution.py:217
  276.5 11.7 %all-to-all-start.6 = ((f32[8,1,1024]{2,1,0:T(1,128)}), f32[8,1,1024]{2,1,0:T(1,128)S(1)}, u32[]{:S(2)}, u32[]{:S(2)}) async-start(f32[8,1,1024]{2,1,0:T(1,128)} %reshape.755), calls=%async_computation.6 | async-start | bytes 65536 | tf_op jit(solution)/shard_map/all_to_all | solution.py:218
  281.5 217.2 %reduce-scatter.5.cloned.1.call-start = ((), (), s32[]{:S(2)}) async-start(), calls=%async_computation.11 | async-start | bytes 5242880 | tf_op jit(solution)/shard_map/reduce_scatter | solution.py:229
  335.8 162.9 %reduce-scatter.3.cloned.1.call-start = ((), (), s32[]{:S(2)}) async-start(), calls=%async_computation.10 | async-start | bytes 5242880 | tf_op jit(solution)/shard_map/reduce_scatter | solution.py:226
  378.9 2.7 copy-start
  383.6 8.7 %copy-start.6 = (bf16[1,768,512]{1,2,0:T(8,128)(2,1)S(1)}, bf16[1,768,512]{1,2,0:T(8,128)(2,1)}, u32[]{:S(2)}) copy-start(bf16[1,768,512]{1,2,0:T(8,128)(2,1)} %copy-done.5) | copy-start | bytes 2359300
  390.0 9.5 %copy-start.4 = (bf16[1,768,512]{1,2,0:T(8,128)(2,1)S(1)}, bf16[1,768,512]{1,2,0:T(8,128)(2,1)}, u32[]{:S(2)}) copy-start(bf16[1,768,512]{1,2,0:T(8,128)(2,1)} %copy-done.3) | copy-start | bytes 2359300
  397.1 9.4 %copy-start.18 = (bf16[1,1024,512]{2,1,0:T(8,128)(2,1)S(1)}, bf16[1,1024,512]{2,1,0:T(8,128)(2,1)}, u32[]{:S(2)}) copy-start(bf16[1,1024,512]{2,1,0:T(8,128)(2,1)} %copy.296) | copy-start | bytes 3145732
  411.0 7.3 %copy-start.12 = (bf16[1,1024,512]{1,2,0:T(8,128)(2,1)S(1)}, bf16[1,1024,512]{1,2,0:T(8,128)(2,1)}, u32[]{:S(2)}) copy-start(bf16[1,1024,512]{1,2,0:T(8,128)(2,1)} %copy.320) | copy-start | bytes 3145732
  418.3 9.5 %copy-start.10 = (bf16[1,1024,512]{1,2,0:T(8,128)(2,1)S(1)}, bf16[1,1024,512]{1,2,0:T(8,128)(2,1)}, u32[]{:S(2)}) copy-start(bf16[1,1024,512]{1,2,0:T(8,128)(2,1)} %copy.321) | copy-start | bytes 3145732
  427.8 9.3 %copy-start.9 = (bf16[1,1024,512]{1,2,0:T(8,128)(2,1)S(1)}, bf16[1,1024,512]{1,2,0:T(8,128)(2,1)}, u32[]{:S(2)}) copy-start(bf16[1,1024,512]{1,2,0:T(8,128)(2,1)} %copy.322) | copy-start | bytes 3145732
  437.0 9.3 %copy-start.15 = (f32[1,768,512]{2,1,0:T(8,128)S(1)}, f32[1,768,512]{2,1,0:T(8,128)}, u32[]{:S(2)}) copy-start(f32[1,768,512]{2,1,0:T(8,128)} %copy.290) | copy-start | bytes 4718596
  449.1 46.7 %copy-start.2 = (f32[256,512]{1,0:T(8,128)S(1)}, f32[256,512]{1,0:T(8,128)}, u32[]{:S(2)}) copy-start(f32[256,512]{1,0:T(8,128)} %copy-done.1) | copy-start | bytes 1572868
Sparse Core Ops, SparseCore 0:
  335.9 41.8 reduce-scatter.4
  411.1 41.9 reduce-scatter.2
where the time goes:
time: 512 us; the launch traced here: 506 us
  matrix products  189 us (37%)
  local copies, waits for them, and re-layouts  83.6 us (16%)
  other arithmetic  72 us (14%)
  waiting for transfers between devices  65.7 us (13%)
  blocking collectives  46.4 us (9%)
  starting transfers between devices  33.9 us (7%)
  between operations  14.9 us (3%)
    all_to_all x1, blocking collectives, per_device(): lax.all_to_all(query_terms[:, rows_dev:, :].reshape(seq_count, blocks, ca...  46.4 us
    all_to_all x1, waiting for transfers between devices, per_device(): lax.all_to_all(pack_rows(query_rows), 'ctx', split_axis=1, concat_axis=1,...  45 us
    convert_element_type x1, other arithmetic, block_gradients(): (probabilities * (products - shift_part[..., None])).astype(jnp.bfloat16)  42.9 us
    dot_general x3, matrix products, block_statistics(): jnp.einsum('srhd,skhd->shrk', head_part(grads_out, start_col, group_heads...  42.8 us
    dot_general x4, matrix products, block_gradients(): jnp.einsum('shrk,srhd->skhd', prob_low, grad_part, preferred_element_type...  33.8 us
    unnamed x80, local copies, waits for them, and re-layouts  26.3 us
    dot_general x1, matrix products, block_gradients(): jnp.einsum('srhd,skhd->shrk', grad_part, value_part, preferred_element_ty...  24.9 us
    slice x10, local copies, waits for them, and re-layouts, head_part(): sliced = matrix[:, :, start_col:start_col + group_heads * HEAD_DIM]  24.9 us
  transfers between devices with their start and end apart: 9, of which 6 were waited for; matrix products, arithmetic and copies ran while one was open for 35% of the time, Pallas kernels for 0%

commit v1 on v0

v1 whole, which is shorter than its diff:
```python
import functools

import jax
import jax.numpy as jnp
from jax import lax
from jax.experimental import pallas as pl
from jax.experimental.pallas import tpu as pltpu
from jax.sharding import PartitionSpec as P

HEAD_DIM = 128
LANES = 128
GROUP_HEADS = 4
NEGATIVE = -1e30
LOG2E = 1.4426950408889634
F32 = jnp.float32
BF16 = jnp.bfloat16


def dot_nt(left, right):
    return lax.dot_general(left, right, (((1,), (1,)), ((), ())), preferred_element_type=F32)


def dot_nn(left, right):
    return lax.dot_general(left, right, (((1,), (0,)), ((), ())), preferred_element_type=F32)


def three_parts(value):
    high = value.astype(BF16).astype(F32)
    rest = value - high
    middle = rest.astype(BF16).astype(F32)
    return jnp.concatenate([high, middle, rest - middle], axis=0).astype(BF16)


def add_parts(value, count):
    return value[:count] + value[count : 2 * count] + value[2 * count :]


def kernel(
    blocks,
    helpers,
    q_ref,
    k_ref,
    v_ref,
    do_ref,
    pick_slots,
    pick_rows,
    select_ref,
    present_ref,
    dq_out,
    dk_out,
    dv_out,
    send_buf,
    recv_buf,
    own_stat,
    stat_blk,
    back_buf,
    log_send,
    log_recv,
    fin_own,
    slot_stat,
    dq_own,
    ret_send,
    ret_recv,
    kv_part,
    sib_recv,
    pair_send,
    pair_recv,
    fwd_s,
    fwd_r,
    stat_s,
    stat_r,
    log_s,
    log_r,
    ret_s,
    ret_r,
    sib_s,
    sib_r,
    pair_s,
    pair_r,
):
    me = lax.axis_index("ctx")
    helper = lax.axis_index("help")
    core = lax.rem(helper, 2)
    xpos = lax.div(helper, 2)
    nx = helpers // 2
    groups = send_buf.shape[0]
    cap = send_buf.shape[3]
    width = send_buf.shape[4]
    heads = width // HEAD_DIM
    rows = q_ref.shape[0]
    keys = k_ref.shape[0]
    slots = blocks * cap
    per_blk = LANES // cap
    tile = 2 * LANES
    tiles = slots // tile
    scaling = HEAD_DIM**-0.5
    scale2 = scaling * LOG2E

    def fwd_copy(g, src, dst):
        return pltpu.make_async_remote_copy(
            send_buf.at[g, dst], recv_buf.at[g, src], fwd_s.at[g, dst], fwd_r.at[g, src],
            device_id={"ctx": dst}, device_id_type=pl.DeviceIdType.MESH,
        )

    def stat_copy(g, src, dst):
        return pltpu.make_async_remote_copy(
            stat_blk.at[g, lax.div(dst, per_blk)], back_buf.at[g, src], stat_s.at[g, dst], stat_r.at[g, src],
            device_id={"ctx": dst}, device_id_type=pl.DeviceIdType.MESH,
        )

    def log_copy(g, src, dst):
        return pltpu.make_async_remote_copy(
            log_send.at[g, dst], log_recv.at[g, src], log_s.at[g, dst], log_r.at[g, src],
            device_id={"ctx": dst}, device_id_type=pl.DeviceIdType.MESH,
        )

    def ret_copy(g, src, dst):
        return pltpu.make_async_remote_copy(
            ret_send.at[g, dst], ret_recv.at[g, src], ret_s.at[g, dst], ret_r.at[g, src],
            device_id={"ctx": dst}, device_id_type=pl.DeviceIdType.MESH,
        )

    def sib_copy(g):
        return pltpu.make_async_remote_copy(
            kv_part.at[g, :, :, 1 - core], sib_recv.at[g], sib_s.at[g], sib_r.at[g],
            device_id={"help": xpos * 2 + 1 - core}, device_id_type=pl.DeviceIdType.MESH,
        )

    def pair_copy(g, src, dst):
        return pltpu.make_async_remote_copy(
            pair_send.at[g, dst], pair_recv.at[g, src], pair_s.at[g, dst], pair_r.at[g, src],
            device_id={"help": dst * 2 + core}, device_id_type=pl.DeviceIdType.MESH,
        )

    def lower(body):
        lax.fori_loop(0, me, lambda i, c: (body(me - 1 - i), c)[1], 0)

    def upper(body):
        lax.fori_loop(me + 1, blocks, lambda i, c: (body(i), c)[1], 0)

    barrier = pltpu.get_barrier_semaphore()

    def greet_ctx(d):
        pl.semaphore_signal(barrier, inc=1, device_id={"ctx": d}, device_id_type=pl.DeviceIdType.MESH)

    lower(greet_ctx)
    upper(greet_ctx)
    pl.semaphore_signal(
        barrier, inc=1, device_id={"help": xpos * 2 + 1 - core}, device_id_type=pl.DeviceIdType.MESH
    )
    for o in range(1, nx):
        pl.semaphore_signal(
            barrier, inc=1, device_id={"help": lax.rem(xpos + o, nx) * 2 + core},
            device_id_type=pl.DeviceIdType.MESH,
        )
    pl.semaphore_wait(barrier, blocks - 1 + nx)

    def pack(g, carry):
        cols = pl.ds(pl.multiple_of(g * width, width), width)
        for which, ref in ((0, q_ref), (1, do_ref)):
            packed = dot_nn(pick_slots[...], ref[:, cols]).astype(BF16)
            send_buf[g, :, which] = packed.reshape(blocks, cap, width)
        lower(lambda d: fwd_copy(g, me, d).start())
        return carry

    lax.fori_loop(0, groups, pack, 0)

    def clear(d, carry):
        @pl.when(d <= me)
        def _():
            def each(g, c):
                recv_buf[g, d] = jnp.zeros(recv_buf.shape[2:], BF16)
                log_recv[g, d] = jnp.zeros(log_recv.shape[2:], F32)
                return c

            lax.fori_loop(0, groups, each, 0)

        @pl.when(d >= me)
        def _():
            def each(g, c):
                back_buf[g, d] = jnp.zeros(back_buf.shape[2:], F32)
                ret_recv[g, d] = jnp.zeros(ret_recv.shape[2:], BF16)
                return c

            lax.fori_loop(0, groups, each, 0)

        return carry

    lax.fori_loop(0, blocks, clear, 0)

    def own_mask():
        row_at = helper * rows + lax.broadcasted_iota(jnp.int32, (keys, rows), 1)
        return lax.broadcasted_iota(jnp.int32, (keys, rows), 0) <= row_at

    def columns(g, h):
        return pl.ds(pl.multiple_of(g * width + h * HEAD_DIM, HEAD_DIM), HEAD_DIM)

    def inner(h):
        return pl.ds(pl.multiple_of(h * HEAD_DIM, HEAD_DIM), HEAD_DIM)

    per_tile = tile // cap

    def routed(g, j, which, h):
        return recv_buf[g, j * per_tile : (j + 1) * per_tile, which, :, inner(h)].reshape(tile, HEAD_DIM)

    def statistics(g):
        upper(lambda s: fwd_copy(g, s, me).wait_recv())

        def head(h, carry):
            key = k_ref[:, columns(g, h)]
            value = v_ref[:, columns(g, h)]

            def local(query, grad, mask):
                scores = dot_nt(key, query) * scale2
                if mask:
                    scores = jnp.where(own_mask(), scores, NEGATIVE)
                top = jnp.max(scores, axis=0, keepdims=True)
                weights = jnp.exp2(scores - top)
                products = dot_nt(value, grad)
                total = jnp.sum(weights, axis=0, keepdims=True)
                center = jnp.sum(weights * products, axis=0, keepdims=True) / total
                return top + jnp.log2(total), center

            log_part, center = local(q_ref[:, columns(g, h)], do_ref[:, columns(g, h)], True)
            own_stat[g, pl.ds(h, 1), :] = log_part
            own_stat[g, pl.ds(heads + h, 1), :] = center
            for j in range(tiles):
                log_part, center = local(routed(g, j, 0, h), routed(g, j, 1, h), False)
                for half in range(2):
                    lanes = slice(half * LANES, (half + 1) * LANES)
                    stat_blk[g, 2 * j + half, pl.ds(h, 1), :] = log_part[:, lanes]
                    stat_blk[g, 2 * j + half, pl.ds(heads + h, 1), :] = center[:, lanes]
            return carry

        lax.fori_loop(0, heads, head, 0)
        upper(lambda s: stat_copy(g, me, s).start())

    def totals(g):
        lower(lambda d: stat_copy(g, d, me).wait_recv())
        count = 2 * heads
        gathered = three_parts(jnp.concatenate([back_buf[g, d] for d in range(blocks)], axis=1))
        logs = [own_stat[g, :heads]]
        centers = [own_stat[g, heads:]]
        for r in range(select_ref.shape[0]):
            got = add_parts(dot_nn(gathered, select_ref[r]), count)
            logs.append(jnp.where(present_ref[r : r + 1, :] > 0, got[:heads], NEGATIVE))
            centers.append(got[heads:])
        top = functools.reduce(jnp.maximum, logs)
        total = sum(jnp.exp2(part - top) for part in logs)
        log_total = top + jnp.log2(total)
        centering = sum(jnp.exp2(part - top) * c for part, c in zip(logs, centers)) / total
        final = jnp.concatenate([log_total, centering], axis=0)
        fin_own[g] = final
        parts = three_parts(final)
        both = select_ref[0]
        for r in range(1, select_ref.shape[0]):
            both = both + select_ref[r]
        spread = add_parts(dot_nt(parts, both), count)
        for d in range(blocks):
            log_send[g, d] = spread[:, d * LANES : (d + 1) * LANES]
        lower(lambda d: log_copy(g, me, d).start())

    def gradients(g):
        upper(lambda s: log_copy(g, s, me).wait_recv())
        for b in range(slots // LANES):
            slot_stat[:, b * LANES : (b + 1) * LANES] = sum(
                log_recv[g, b * per_blk + i] for i in range(per_blk)
            )

        def head(h, carry):
            key = k_ref[:, columns(g, h)]
            value = v_ref[:, columns(g, h)]
            key_turned = key.T

            def local(query, grad, log_row, center, mask):
                scores = dot_nt(key, query) * scale2
                probs = jnp.exp2(scores - log_row)
                if mask:
                    probs = jnp.where(own_mask(), probs, 0.0)
                products = dot_nt(value, grad)
                mixed = (probs * (products - center)).astype(BF16)
                dv = dot_nn(probs.astype(BF16), grad)
                dk = dot_nn(mixed, query)
                dq = (dot_nn(key_turned, mixed) * scaling).T
                return dq, dk, dv

            dq, dk, dv = local(
                q_ref[:, columns(g, h)],
                do_ref[:, columns(g, h)],
                fin_own[g, pl.ds(h, 1), :],
                fin_own[g, pl.ds(heads + h, 1), :],
                True,
            )
            dq_own[:, columns(g, h)] = dq
            for j in range(tiles):
                lanes = slice(j * tile, (j + 1) * tile)
                dq, dk_new, dv_new = local(
                    routed(g, j, 0, h),
                    routed(g, j, 1, h),
                    slot_stat[pl.ds(h, 1), lanes],
                    slot_stat[pl.ds(heads + h, 1), lanes],
                    False,
                )
                dk = dk + dk_new
                dv = dv + dv_new
                ret_send[g, j * per_tile : (j + 1) * per_tile, :, inner(h)] = dq.astype(BF16).reshape(
                    per_tile, cap, HEAD_DIM
                )
            shape = (nx, 2, rows, HEAD_DIM)
            kv_part[g, 0, :, :, :, inner(h)] = (dk * scaling).astype(BF16).reshape(shape)
            kv_part[g, 1, :, :, :, inner(h)] = dv.astype(BF16).reshape(shape)
            return carry

        lax.fori_loop(0, heads, head, 0)
        upper(lambda s: ret_copy(g, me, s).start())
        sib_copy(g).start()

    def pair_sums(g):
        sib_copy(g).wait_recv()
        for o in range(1, nx):
            other = lax.rem(xpos + o, nx)
            pair_send[g, other] = (
                kv_part[g, :, other, core].astype(F32) + sib_recv[g, :, other].astype(F32)
            ).astype(BF16)
            pair_copy(g, xpos, other).start()

    def finish(g):
        cols = pl.ds(pl.multiple_of(g * width, width), width)
        total = kv_part[g, :, xpos, core].astype(F32) + sib_recv[g, :, xpos].astype(F32)
        for o in range(1, nx):
            other = lax.rem(xpos + o, nx)
            pair_copy(g, other, xpos).wait_recv()
            total = total + pair_recv[g, other].astype(F32)
        dk_out[:, cols] = total[0].astype(BF16)
        dv_out[:, cols] = total[1].astype(BF16)
        lower(lambda d: ret_copy(g, d, me).wait_recv())
        terms = dot_nn(pick_rows[...], ret_recv[g].reshape(slots, width))
        dq_out[:, cols] = (dq_own[:, cols] + terms).astype(BF16)

    def step(i, carry):
        @pl.when((i >= 1) & (i < groups + 1))
        def _():
            totals(i - 1)

        @pl.when(i < groups)
        def _():
            statistics(i)

        @pl.when((i >= 1) & (i < groups + 1))
        def _():
            gradients(i - 1)

        @pl.when((i >= 2) & (i < groups + 2))
        def _():
            pair_sums(i - 2)

        @pl.when(i >= 3)
        def _():
            finish(i - 3)

        return carry

    lax.fori_loop(0, groups + 3, step, 0)

    def drain(g, carry):
        lower(lambda d: fwd_copy(g, me, d).wait_send())
        upper(lambda s: stat_copy(g, me, s).wait_send())
        lower(lambda d: log_copy(g, me, d).wait_send())
        upper(lambda s: ret_copy(g, me, s).wait_send())
        sib_copy(g).wait_send()
        for o in range(1, nx):
            pair_copy(g, xpos, lax.rem(xpos + o, nx)).wait_send()
        return carry

    lax.fori_loop(0, groups, drain, 0)


def per_device(blocks, helpers, query_rows, key_rows, value_rows, output_grad, block_choice):
    me = lax.axis_index("ctx")
    rows, features = query_rows.shape[1:]
    routes = block_choice.shape[2]
    keys = key_rows.shape[1]
    cap = max(16, 2 * max(1, rows // blocks))
    slots = blocks * cap
    width = min(GROUP_HEADS * HEAD_DIM, features)
    groups = features // width
    heads = width // HEAD_DIM
    nx = helpers // 2

    choice = block_choice[0].T
    present = choice < me
    targets = jnp.where(present, me - 1 - choice, -1)
    matches = (targets[:, None, :] == jnp.arange(blocks, dtype=jnp.int32)[None, :, None]).astype(jnp.int32)
    counts = jnp.sum(matches, axis=0)
    upto = (
        jnp.arange(rows, dtype=jnp.int32)[:, None] < jnp.arange(rows, dtype=jnp.int32)[None, :]
    ).astype(BF16)
    earlier = jnp.dot(counts.astype(BF16), upto, preferred_element_type=F32).astype(jnp.int32)
    places = jnp.sum(matches * earlier[None], axis=1)
    slot_ids = jnp.where(present, targets * cap + places, -1)
    slot_iota = jnp.arange(slots, dtype=jnp.int32)
    pick_slots = jnp.any(slot_ids[:, None, :] == slot_iota[None, :, None], axis=0).astype(BF16)
    pick_rows = jnp.any(slot_ids[:, :, None] == slot_iota[None, None, :], axis=0).astype(BF16)
    lane_ids = jnp.where(present, targets * LANES + lax.rem(me * cap, LANES) + places, -1)
    select = (lane_ids[:, None, :] == jnp.arange(blocks * LANES, dtype=jnp.int32)[None, :, None]).astype(BF16)

    count = 2 * heads
    dma = pltpu.SemaphoreType.DMA
    vmem = pl.BlockSpec(memory_space=pltpu.VMEM)
    out = jax.ShapeDtypeStruct((rows, features), BF16)
    dq, dk, dv = pl.pallas_call(
        functools.partial(kernel, blocks, helpers),
        out_shape=(out, out, out),
        in_specs=[vmem] * 8,
        out_specs=(vmem, vmem, vmem),
        scratch_shapes=[
            pltpu.VMEM((groups, blocks, 2, cap, width), BF16),
            pltpu.VMEM((groups, blocks, 2, cap, width), BF16),
            pltpu.VMEM((groups, count, rows), F32),
            pltpu.VMEM((groups, slots // LANES, count, LANES), F32),
            pltpu.VMEM((groups, blocks, count, LANES), F32),
            pltpu.VMEM((groups, blocks, count, LANES), F32),
            pltpu.VMEM((groups, blocks, count, LANES), F32),
            pltpu.VMEM((groups, count, rows), F32),
            pltpu.VMEM((count, slots), F32),
            pltpu.VMEM((rows, features), F32),
            pltpu.VMEM((groups, blocks, cap, width), BF16),
            pltpu.VMEM((groups, blocks, cap, width), BF16),
            pltpu.VMEM((groups, 2, nx, 2, rows, width), BF16),
            pltpu.VMEM((groups, 2, nx, rows, width), BF16),
            pltpu.VMEM((groups, nx, 2, rows, width), BF16),
            pltpu.VMEM((groups, nx, 2, rows, width), BF16),
        ]
        + [dma((groups, blocks))] * 8
        + [dma((groups,))] * 2
        + [dma((groups, nx))] * 2,
        compiler_params=pltpu.CompilerParams(
            collective_id=0, has_side_effects=True, vmem_limit_bytes=60 * 1024 * 1024
        ),
        name="routed_attention_grad",
    )(
        query_rows[0],
        key_rows[0],
        value_rows[0],
        output_grad[0],
        pick_slots,
        pick_rows,
        select,
        present.astype(jnp.int32),
    )
    return dq[None], dk[None], dv[None]


def solution(mesh):
    rows = P(None, ("ctx", "help"), None)
    block = P(None, "ctx", None)
    return jax.shard_map(
        functools.partial(per_device, mesh.shape["ctx"], mesh.shape["help"]),
        mesh=mesh,
        in_specs=(rows, block, block, rows, rows),
        out_specs=(rows, rows, rows),
        check_vma=False,
    )
```

time: 512 us -> 198 us (0.39); the launches traced: 506 us -> 198 us
  matrix products: 189 us -> 0.15 us
  Pallas kernels: 0 us -> 186 us
  local copies, waits for them, and re-layouts: 83.6 us -> 5.67 us
  other arithmetic: 72 us -> 5.11 us
  waiting for transfers between devices: 65.7 us -> 0 us
  blocking collectives: 46.4 us -> 0 us
  starting transfers between devices: 33.9 us -> 0 us
  between operations: 14.9 us -> 0.68 us
    dot_general x31 -> x1, matrix products: 189 us -> 0.15 us  [per_device(): jnp.dot(counts.astype(BF16), upto, preferred_element_type=F32)]
    pallas_call x0 -> x1, Pallas kernels: none -> 186 us  [per_device(): pl.pallas_call(functools.partial(kernel, blocks, helpers), out_shape=(out...]
    all_to_all x7 -> x0, waiting for transfers between devices: 65.7 us -> none  [the longest x1 45 us: per_device(): lax.all_to_all(pack_rows(query_rows), 'ctx', split_axis=1, concat_axis=1,...]
    all_to_all x1 -> x0, blocking collectives: 46.4 us -> none  [per_device(): lax.all_to_all(query_terms[:, rows_dev:, :].reshape(seq_count, blocks, ca...]
    convert_element_type x1 -> x4, other arithmetic: 42.9 us -> 4.04 us  [the longest x1 1.32 us: per_device(): (lane_ids[:, None, :] == jnp.arange(blocks * LANES, dtype=jnp.int32)[None...]
    all_to_all x7 -> x0, starting transfers between devices: 33.6 us -> none  [the longest x1 7.28 us: per_device(): lax.all_to_all(pack_rows(query_rows), 'ctx', split_axis=1, concat_axis=1,...]
    slice x13 -> x0, local copies, waits for them, and re-layouts: 25.9 us -> none  [the longest x10 24.9 us: head_part(): sliced = matrix[:, :, start_col:start_col + group_heads * HEAD_DIM]]
    unnamed x80 -> x5, local copies, waits for them, and re-layouts: 26.3 us -> 5.67 us
  transfers between devices with their start and end apart: 9 -> 0, of which waited for: 6 -> 0; matrix products, arithmetic and copies ran while one was open for 35% -> 0% of each run, Pallas kernels for 0% -> 0%
where the time goes in v1:
time: 198 us
  Pallas kernels  186 us (94%)
  local copies, waits for them, and re-layouts  5.67 us (3%)
  other arithmetic  5.11 us (3%)
    pallas_call x1, Pallas kernels, per_device(): pl.pallas_call(functools.partial(kernel, blocks, helpers), out_shape=(out...  186 us
    unnamed x5, local copies, waits for them, and re-layouts  5.67 us

profile of v1, /device:TPU:0, one launch (start us, length us, event | category | flops | bytes accessed | tf_op | source)
XLA Modules:
  0.0 197.5 jit_solution(12698507248286487315)
XLA Ops:
  0.6 1.3 bitcast_convert_fusion
  1.9 0.7 bitcast_select_fusion.2
  2.6 0.2 convolution_convert_fusion
  2.8 0.2 fusion.2
  2.9 0.2 fusion.1
  3.1 0.7 convert_element_type.25.pick_slots
  3.9 0.7 convert_element_type.26.pick_rows
  4.6 1.3 fusion.select_ref
  5.9 185.9 %routed_attention_grad.1 = (bf16[256,2048]{1,0:T(8,128)(2,1)}, bf16[256,2048]{1,0:T(8,128)(2,1)}, bf16[256,2048]{1,0:T(8,128)(2,1)}) custom-call(bf16[256,2048]{1,0:T(8,128)(2,1)} %bitcast.20, bf16[1024,2048]{1,0:T(8,128)(2,1)} %bitcast.18, bf16[1024,2048]{1,0:T(8,128)(2,1)} %bitcast.19, bf16[256,2048]{1,0:T(8,128)(2,1)} %bitcast.21, ...), custom_call_target="tpu_custom_call" | custom-call | tf_op jit(solution)/shard_map/routed_attention_grad/pallas_call | solution.py:411
  191.8 0.0 copy-start
  191.9 2.4 %copy.11 = bf16[1,256,2048]{2,1,0:T(8,128)(2,1)} copy(bf16[1,256,2048]{2,1,0:T(8,128)(2,1)} %bitcast.24) | data formatting | bytes 2097152
  194.2 2.3 %copy.12 = bf16[1,256,2048]{2,1,0:T(8,128)(2,1)} copy(bf16[1,256,2048]{2,1,0:T(8,128)(2,1)} %bitcast.23) | data formatting | bytes 2097152
  196.6 0.0 copy-done
  196.6 1.0 copy.13
  (3 shorter events, 0.0 us)
Async XLA Ops:
  191.8 4.7 %copy-start = (bf16[256,2048]{1,0:T(8,128)(2,1)S(1)}, bf16[256,2048]{1,0:T(8,128)(2,1)}, u32[]{:S(2)}) copy-start(bf16[256,2048]{1,0:T(8,128)(2,1)} %get-tuple-element.8) | copy-start | bytes 3145732

commit v2 on v1

--- a/solution.py
+++ b/solution.py
@@ -9,7 +9,8 @@
 
 HEAD_DIM = 128
 LANES = 128
-GROUP_HEADS = 4
+GROUP_HEADS = 2
+AHEAD = 2
 NEGATIVE = -1e30
 LOG2E = 1.4426950408889634
 F32 = jnp.float32
@@ -163,7 +164,7 @@
         lower(lambda d: fwd_copy(g, me, d).start())
         return carry
 
-    lax.fori_loop(0, groups, pack, 0)
+    lax.fori_loop(0, min(AHEAD, groups), pack, 0)
 
     def clear(d, carry):
         @pl.when(d <= me)
@@ -341,6 +342,10 @@
         @pl.when((i >= 1) & (i < groups + 1))
         def _():
             totals(i - 1)
+
+        @pl.when(i + AHEAD < groups)
+        def _():
+            pack(i + AHEAD, 0)
 
         @pl.when(i < groups)
         def _():

time: 198 us -> 161 us (0.81)
  Pallas kernels: 186 us -> 149 us
    pallas_call x1, Pallas kernels: 186 us -> 149 us  [per_device(): pl.pallas_call(functools.partial(kernel, blocks, helpers), out_shape=(out...]
where the time goes in v2:
time: 161 us
  Pallas kernels  149 us (93%)
  local copies, waits for them, and re-layouts  5.67 us (4%)
  other arithmetic  5.11 us (3%)
    pallas_call x1, Pallas kernels, per_device(): pl.pallas_call(functools.partial(kernel, blocks, helpers), out_shape=(out...  149 us
    unnamed x5, local copies, waits for them, and re-layouts  5.67 us

profile of v2, /device:TPU:0, one launch (start us, length us, event | category | flops | bytes accessed | tf_op | source)
XLA Modules:
  0.0 161.0 jit_solution(1896167447679642037)
XLA Ops:
  0.6 1.3 bitcast_convert_fusion
  1.9 0.7 bitcast_select_fusion.2
  2.6 0.2 convolution_convert_fusion
  2.8 0.2 fusion.2
  2.9 0.2 fusion.1
  3.1 0.7 convert_element_type.25.pick_slots
  3.9 0.7 convert_element_type.26.pick_rows
  4.6 1.3 fusion.select_ref
  5.9 149.4 %routed_attention_grad.1 = (bf16[256,2048]{1,0:T(8,128)(2,1)}, bf16[256,2048]{1,0:T(8,128)(2,1)}, bf16[256,2048]{1,0:T(8,128)(2,1)}) custom-call(bf16[256,2048]{1,0:T(8,128)(2,1)} %bitcast.20, bf16[1024,2048]{1,0:T(8,128)(2,1)} %bitcast.18, bf16[1024,2048]{1,0:T(8,128)(2,1)} %bitcast.19, bf16[256,2048]{1,0:T(8,128)(2,1)} %bitcast.21, ...), custom_call_target="tpu_custom_call" | custom-call | tf_op jit(solution)/shard_map/routed_attention_grad/pallas_call | solution.py:416
  155.3 0.0 copy-start
  155.4 2.4 %copy.11 = bf16[1,256,2048]{2,1,0:T(8,128)(2,1)} copy(bf16[1,256,2048]{2,1,0:T(8,128)(2,1)} %bitcast.24) | data formatting | bytes 2097152
  157.8 2.3 %copy.12 = bf16[1,256,2048]{2,1,0:T(8,128)(2,1)} copy(bf16[1,256,2048]{2,1,0:T(8,128)(2,1)} %bitcast.23) | data formatting | bytes 2097152
  160.1 0.0 copy-done
  160.1 1.0 copy.13
  (3 shorter events, 0.0 us)
Async XLA Ops:
  155.3 4.7 %copy-start = (bf16[256,2048]{1,0:T(8,128)(2,1)S(1)}, bf16[256,2048]{1,0:T(8,128)(2,1)}, u32[]{:S(2)}) copy-start(bf16[256,2048]{1,0:T(8,128)(2,1)} %get-tuple-element.8) | copy-start | bytes 3145732

commit v3 on v2

--- a/solution.py
+++ b/solution.py
@@ -10,7 +10,7 @@
 HEAD_DIM = 128
 LANES = 128
 GROUP_HEADS = 2
-AHEAD = 2
+AHEAD = 1
 NEGATIVE = -1e30
 LOG2E = 1.4426950408889634
 F32 = jnp.float32

time: 161 us -> 154 us (0.957)
  Pallas kernels: 149 us -> 142 us
    pallas_call x1, Pallas kernels: 149 us -> 142 us  [per_device(): pl.pallas_call(functools.partial(kernel, blocks, helpers), out_shape=(out...]
where the time goes in v3:
time: 154 us
  Pallas kernels  142 us (92%)
  local copies, waits for them, and re-layouts  5.67 us (4%)
  other arithmetic  5.11 us (3%)
    pallas_call x1, Pallas kernels, per_device(): pl.pallas_call(functools.partial(kernel, blocks, helpers), out_shape=(out...  142 us
    unnamed x5, local copies, waits for them, and re-layouts  5.67 us

profile of v3, /device:TPU:0, one launch (start us, length us, event | category | flops | bytes accessed | tf_op | source)
XLA Modules:
  0.0 153.8 jit_solution(14984169180116576099)
XLA Ops:
  0.6 1.3 bitcast_convert_fusion
  1.9 0.7 bitcast_select_fusion.2
  2.6 0.2 convolution_convert_fusion
  2.8 0.2 fusion.2
  2.9 0.2 fusion.1
  3.1 0.7 convert_element_type.25.pick_slots
  3.9 0.7 convert_element_type.26.pick_rows
  4.6 1.3 fusion.select_ref
  5.9 142.2 %routed_attention_grad.1 = (bf16[256,2048]{1,0:T(8,128)(2,1)}, bf16[256,2048]{1,0:T(8,128)(2,1)}, bf16[256,2048]{1,0:T(8,128)(2,1)}) custom-call(bf16[256,2048]{1,0:T(8,128)(2,1)} %bitcast.20, bf16[1024,2048]{1,0:T(8,128)(2,1)} %bitcast.18, bf16[1024,2048]{1,0:T(8,128)(2,1)} %bitcast.19, bf16[256,2048]{1,0:T(8,128)(2,1)} %bitcast.21, ...), custom_call_target="tpu_custom_call" | custom-call | tf_op jit(solution)/shard_map/routed_attention_grad/pallas_call | solution.py:416
  148.1 0.0 copy-start
  148.2 2.4 %copy.11 = bf16[1,256,2048]{2,1,0:T(8,128)(2,1)} copy(bf16[1,256,2048]{2,1,0:T(8,128)(2,1)} %bitcast.24) | data formatting | bytes 2097152
  150.6 2.3 %copy.12 = bf16[1,256,2048]{2,1,0:T(8,128)(2,1)} copy(bf16[1,256,2048]{2,1,0:T(8,128)(2,1)} %bitcast.23) | data formatting | bytes 2097152
  152.9 0.0 copy-done
  152.9 1.0 copy.13
  (3 shorter events, 0.0 us)
Async XLA Ops:
  148.1 4.7 %copy-start = (bf16[256,2048]{1,0:T(8,128)(2,1)S(1)}, bf16[256,2048]{1,0:T(8,128)(2,1)}, u32[]{:S(2)}) copy-start(bf16[256,2048]{1,0:T(8,128)(2,1)} %get-tuple-element.8) | copy-start | bytes 3145732
